TPU v7x, 512 devices: a whole 4x8x8 slice. The times are simulated.
512 devices in a mesh: row: 32 (over y, z_lo), col: 16 (over x, z_hi, core).
Axes of the slice: x: 4, y: 8, z: 8 (z_hi: 2, z_lo: 4; z = z_hi * 4 + z_lo), core: 2. Of those that a mesh axis runs over, the one named last changes fastest.
Arguments:
- occ_orbitals: bfloat16 [8192, 2048], P(('row', 'col')), may hold values from -2 to 2
- vir_orbitals: bfloat16 [8192, 1024], P(('row', 'col')), may hold values from -2.5 to 2.5
- occ_energy: float32 [2048], replicated, may hold values from -2 to -0.1
- vir_energy: float32 [1024], replicated, may hold values from 0.1 to 2.5
- tau_points: float32 [2], replicated, may hold values from 0.3 to 1.5
Outputs:
- chi0: float32 [2, 8192, 8192], P(None, 'row', 'col')
All inputs are finite; a program needn't handle non-finite values.
Results may differ from a plain program's by a relative error of at most 0.00047.
Values may be sent and summed in bfloat16 or wider, within the bound.
A program may use at most 64 MiB of HBM per device.

v0:
```python
import jax
import jax.numpy as jnp
from jax import lax
from jax.sharding import PartitionSpec as P

NOCC = 2048
NTAU = 2


def from_root(shard, axis, root):
    mine = lax.axis_index(axis) == root
    return lax.psum(jnp.where(mine, shard, jnp.zeros_like(shard)), axis)


def weighted_side(row_panel, occ_energy, vir_energy, tau_points):
    occ_scales = jnp.exp(tau_points[:, None] * occ_energy[None, :])
    vir_scales = jnp.exp(-tau_points[:, None] * vir_energy[None, :])
    scales = jnp.concatenate([occ_scales, vir_scales], axis=1)
    weighted = (row_panel[None].astype(jnp.float32) * scales[:, None, :]).astype(jnp.bfloat16)
    return weighted.reshape(-1, row_panel.shape[1])


def tile_values(weighted, columns, row_count):
    contract = (((1,), (1,)), ((), ()))
    gram_occ = lax.dot_general(
        weighted[:, :NOCC], columns[:, :NOCC], contract, preferred_element_type=jnp.float32
    )
    gram_vir = lax.dot_general(
        weighted[:, NOCC:], columns[:, NOCC:], contract, preferred_element_type=jnp.float32
    )
    return -(gram_occ * gram_vir).reshape(NTAU, row_count, columns.shape[0])


def local(occ_orbitals, vir_orbitals, occ_energy, vir_energy, tau_points):
    combined = jnp.concatenate([occ_orbitals, vir_orbitals], axis=1)
    row_panel = lax.all_gather(combined, "col", axis=0, tiled=True)
    row_count = row_panel.shape[0]
    weighted = weighted_side(row_panel, occ_energy, vir_energy, tau_points)
    half_count = lax.axis_size("row") // lax.axis_size("col")
    root_base = half_count * lax.axis_index("col")
    halves = []
    for which_half in range(half_count):
        halves.append(from_root(row_panel, "row", root_base + which_half))
    columns = jnp.concatenate(halves, axis=0)
    polar = tile_values(weighted, columns, row_count)
    return polar


def solution(mesh):
    placed = (P(("row", "col"), None), P(("row", "col"), None), P(), P(), P())
    return jax.shard_map(
        local, mesh=mesh, in_specs=placed, out_specs=P(None, "row", "col"), check_vma=False
    )
```

profile of v0, /device:TPU:6, one launch (start us, length us, event | category | flops | bytes accessed | tf_op | source)
XLA Modules:
  0.0 415.2 jit_solution(4973585393043382241)
XLA Ops:
  6.5 0.0 all-gather.2.cloned.1.call-start
  6.5 1.5 pad_maximum_fusion
  8.0 0.0 all-gather.2.cloned.1.call-update
  8.1 0.0 all-reduce.3.cloned.1.call-start
  8.1 71.9 %all-gather.2.cloned.1.call-done = bf16[256,3072]{1,0:T(8,128)(2,1)} async-done(((bf16[16,3072]{1,0:T(8,128)(2,1)}), bf16[256,3072]{1,0:T(8,128)(2,1)}) %all-gather.2.cloned.1.call-update) | async-done | bytes 1572880 | tf_op jit(solution)/shard_map/all_gather | solution.py:36
  80.1 4.0 fusion.6
  84.1 0.0 copy-start.4
  84.1 0.0 copy-start.3
  84.1 0.0 copy-start.2
  84.1 0.0 all-reduce.3.cloned.1.call-update
  84.1 0.6 copy-done.4
  84.7 0.0 copy-done.3
  84.8 0.1 multiply_exponential_fusion.1
  84.9 0.0 copy-done.2
  84.9 0.1 multiply_exponential_fusion
  85.0 2.2 multiply_convert_fusion
  87.2 315.3 %all-reduce.3.cloned.1.call-done = (bf16[256,3072]{1,0:T(8,128)(2,1)}, bf16[256,3072]{1,0:T(8,128)(2,1)}) async-done(((bf16[256,3072]{1,0:T(8,128)(2,1)}, bf16[256,3072]{1,0:T(8,128)(2,1)}), (bf16[256,3072]{1,0:T(8,128)(2,1)}, bf16[256,3072]{1,0:T(8,128)(2,1)})) %all-reduce.3.cloned.1.call-update) | async-done | bytes 3145744 | tf_op jit(solution)/shard_map/psum | solution.py:12
  402.6 0.0 copy-start.1
  402.6 0.0 copy-start
  402.6 1.7 constant_dynamic-update-slice_fusion.1
  404.2 0.2 copy-done.1
  404.4 0.1 constant_dynamic-update-slice_fusion
  404.5 0.8 copy-done
  405.4 1.3 fusion
  406.7 1.7 fusion.3
  (2 shorter events, 0.0 us)
Async XLA Ops:
  6.5 73.5 %all-gather.2.cloned.1.call-start = ((), (), s32[]{:S(2)}) async-start(), calls=%async_computation | async-start | bytes 1671168 | tf_op jit(solution)/shard_map/all_gather | solution.py:36
  8.1 394.5 %all-reduce.3.cloned.1.call-start = ((), (), s32[]{:S(2)}) async-start(), calls=%async_computation.1 | async-start | bytes 6291456 | tf_op jit(solution)/shard_map/psum | solution.py:12
  84.1 0.7 copy-start.4
  84.1 0.7 copy-start.3
  84.1 0.8 copy-start.2
  402.6 1.9 copy-start.1
  402.6 2.8 copy-start
Sparse Core Ops, SparseCore 0:
  10.6 69.4 all-gather.1
  84.2 318.2 all-reduce.2
where the time goes:
time: 416 us; the launch traced here: 415 us
  waiting for transfers between devices  387 us (93%)
  between operations  13.5 us (3%)
  other arithmetic  7.94 us (2%)
    psum x1, waiting for transfers between devices, from_root(): return lax.psum(jnp.where(mine, shard, jnp.zeros_like(shard)), axis)  315 us
    all_gather x1, waiting for transfers between devices, local(): row_panel = lax.all_gather(combined, 'col', axis=0, tiled=True)  71.9 us
  transfers between devices with their start and end apart: 2, of which 2 were waited for; matrix products, arithmetic and copies ran while one was open for 1% of the time, Pallas kernels for 0%

commit v1 on v0

v1 whole, which is shorter than its diff:
```python
import jax
import jax.numpy as jnp
from jax import lax
from jax.experimental import pallas as pl
from jax.experimental.pallas import tpu as pltpu
from jax.sharding import PartitionSpec as P

PIECES = 8
OCC_W = 256
VIR_W = 128
WIDTH = OCC_W + VIR_W
BLOCK = 16
ROWS = 256
COLS = 512
GROUP = 4
CHUNK = COLS // GROUP
NTAU = 2
MESH = pl.DeviceIdType.MESH


def gather_and_multiply(
    occ_ref, vir_ref, occ_energy_ref, vir_energy_ref, tau_ref, out_ref,
    own, rows, cols, scales, total_occ, total_vir,
    land_send, land_recv, near_send, near_recv, up_send, up_recv, down_send, down_recv,
    row_send, row_recv, core_send, core_recv, own_sem,
):
    row, col = lax.axis_index("row"), lax.axis_index("col")
    y, g = row // GROUP, row % GROUP

    flip = (g, g + 1 - 2 * (g % 2), (g + 2) % GROUP, GROUP - 1 - g)
    over = col + 2 - 4 * (col // 2 % 2)

    def near(k):
        return (y * GROUP + flip[k], col)

    above = ((row + GROUP) % (PIECES * GROUP), col)
    below = ((row + (PIECES - 1) * GROUP) % (PIECES * GROUP), col)
    across = (row, over)
    sibling = (row, col + 1 - 2 * (col % 2))

    def beside(k):
        return (row, (col + 4 * k) % 16)

    land_g = (row % 2) * 2 + col // 8
    land_col = row // 2
    source_row = 2 * col + g // 2

    def landing(j):
        return j * GROUP + land_g, land_col

    def source(i):
        return source_row, (g % 2) * 8 + i

    def same(place):
        return jnp.logical_and(place[0] == row, place[1] == col)

    barrier = pltpu.get_barrier_semaphore()
    partners = [near(1), near(2), near(3), above, below, across, sibling, beside(1), beside(2), beside(3)]
    partners += [source(i) for i in range(8)]
    for place in partners:
        pl.semaphore_signal(barrier, inc=1, device_id=place, device_id_type=MESH)
    for j in range(PIECES):
        own[j, :, :OCC_W] = occ_ref[:, j * OCC_W:(j + 1) * OCC_W]
        own[j, :, OCC_W:] = vir_ref[:, j * VIR_W:(j + 1) * VIR_W]
        for t in range(NTAU):
            scales[j, t:t + 1, :OCC_W] = jnp.exp(tau_ref[t] * occ_energy_ref[:, j * OCC_W:(j + 1) * OCC_W])
            scales[j, t:t + 1, OCC_W:] = jnp.exp(-tau_ref[t] * vir_energy_ref[:, j * VIR_W:(j + 1) * VIR_W])

    pl.semaphore_wait(barrier, len(partners))

    def remote(src, dst, send, recv, place):
        return pltpu.make_async_remote_copy(
            src_ref=src, dst_ref=dst, send_sem=send, recv_sem=recv, device_id=place, device_id_type=MESH
        )

    def land_copy(j):
        spot = cols.at[j, pl.ds(pl.multiple_of(land_g * CHUNK + (col % 8) * BLOCK, BLOCK), BLOCK)]
        return remote(own.at[j], spot, land_send.at[j], land_recv, landing(j))

    for j in range(PIECES):
        @pl.when(same(landing(j)))
        def _():
            spot = cols.at[j, pl.ds(pl.multiple_of(land_g * CHUNK + (col % 8) * BLOCK, BLOCK), BLOCK)]
            pltpu.make_async_copy(own.at[j], spot, land_recv).start()

        @pl.when(jnp.logical_not(same(landing(j))))
        def _():
            land_copy(j).start()

    def row_spot(c):
        return rows.at[:, pl.ds(pl.multiple_of(c * BLOCK, BLOCK), BLOCK)]

    def row_copy(which, k):
        src = own if which == 0 else row_spot(over)
        c = col if which == 0 else over
        place = across if k == 0 else beside(k)
        return remote(src, row_spot(c), row_send.at[which, k], row_recv.at[which, k], place)

    def row_arrival(which, k):
        c = over if k == 0 else ((over if which else col) + 16 - 4 * k) % 16
        return c, remote(row_spot(c), row_spot(c), row_send.at[which, k], row_recv.at[which, k], sibling)

    def core_copy(slot, c, src=None):
        return remote(row_spot(c) if src is None else src, row_spot(c), core_send.at[slot], core_recv.at[slot], sibling)

    own_copy = pltpu.make_async_copy(own, row_spot(col), own_sem)
    own_copy.start()
    row_copies = [row_copy(0, k) for k in range(4)]
    core_copies = [core_copy(0, col, own)]
    for copy in row_copies + core_copies:
        copy.start()

    def chunk(j, k):
        return cols.at[j, pl.ds(pl.multiple_of(flip[k] * CHUNK, CHUNK), CHUNK)]

    def up_copy(step, k):
        j = (y + PIECES - step) % PIECES
        return remote(chunk(j, k), chunk(j, k), up_send.at[step, k], up_recv.at[step, k], above)

    def down_copy(step, k):
        j = (y + step) % PIECES
        return remote(chunk(j, k), chunk(j, k), down_send.at[step, k], down_recv.at[step, k], below)

    def up_wait(step, k):
        j = (y + PIECES - step - 1) % PIECES
        remote(chunk(j, k), chunk(j, k), up_send.at[step, k], up_recv.at[step, k], above).wait_recv()

    def down_wait(step, k):
        j = (y + step + 1) % PIECES
        remote(chunk(j, k), chunk(j, k), down_send.at[step, k], down_recv.at[step, k], below).wait_recv()

    ring_copies = []

    def forward(step, k, up, down):
        if up:
            ring_copies.append(up_copy(step, k))
            ring_copies[-1].start()
        if down:
            ring_copies.append(down_copy(step, k))
            ring_copies[-1].start()

    pltpu.make_async_copy(chunk(y, 0), chunk(y, 0), land_recv).wait()
    near_copies = [remote(chunk(y, 0), chunk(y, 0), near_send.at[k], near_recv.at[k], near(k)) for k in range(1, 4)]
    forward(0, 0, True, True)
    for copy in near_copies:
        copy.start()
    for k in range(1, 4):
        remote(chunk(y, k), chunk(y, k), near_send.at[k], near_recv.at[k], near(k)).wait_recv()
        forward(0, k, True, True)

    c, arrival = row_arrival(0, 0)
    arrival.wait_recv()
    second = [row_copy(1, k) for k in range(1, 4)] + [core_copy(1, c)]
    for copy in second:
        copy.start()
    row_copies += second[:3]
    core_copies.append(second[3])

    for k in range(GROUP):
        up_wait(0, k)
        forward(1, k, True, False)
        down_wait(0, k)
        forward(1, k, False, True)

    slot = 2
    for which in range(2):
        for k in (1, 3, 2):
            c, arrival = row_arrival(which, k)
            arrival.wait_recv()
            core_copies.append(core_copy(slot, c))
            core_copies[-1].start()
            slot += 1

    own_copy.wait()
    for at in range(8):
        core_copies[at].wait_recv()

    contract = (((1,), (1,)), ((), ()))

    def grams(j, t):
        panel = rows[j].astype(jnp.float32)
        weighted = (panel * scales[j, pl.ds(t, 1), :]).astype(jnp.bfloat16)
        gram_occ = lax.dot_general(
            weighted[:, :OCC_W], cols[j, :, :OCC_W], contract, preferred_element_type=jnp.float32
        )
        gram_vir = lax.dot_general(
            weighted[:, OCC_W:], cols[j, :, OCC_W:], contract, preferred_element_type=jnp.float32
        )
        return gram_occ, gram_vir

    def accumulate(j, first=False):
        @pl.loop(0, NTAU)
        def _(t):
            gram_occ, gram_vir = grams(j, t)
            if first:
                total_occ[t] = gram_occ
                total_vir[t] = gram_vir
            else:
                total_occ[t] += gram_occ
                total_vir[t] += gram_vir

    accumulate(y, True)
    accumulate((y + 7) % PIECES)
    accumulate((y + 1) % PIECES)

    for step in (1, 2):
        for k in range(GROUP):
            up_wait(step, k)
            forward(step + 1, k, step < 2 or k < 2, False)
            down_wait(step, k)
            forward(step + 1, k, False, step < 2 or k >= 2)
        accumulate((y + 7 - step) % PIECES)
        accumulate((y + 1 + step) % PIECES)

    for k in range(2):
        up_wait(3, k)
        down_wait(3, k + 2)

    last = (y + 4) % PIECES
    for t in range(NTAU):
        gram_occ, gram_vir = grams(last, t)
        out_ref[t] = -((total_occ[t] + gram_occ) * (total_vir[t] + gram_vir))

    for copy in ring_copies + near_copies + row_copies + core_copies:
        copy.wait_send()
    for j in range(PIECES):
        @pl.when(jnp.logical_not(same(landing(j))))
        def _():
            land_copy(j).wait_send()


def local(occ_orbitals, vir_orbitals, occ_energy, vir_energy, tau_points):
    dma = pltpu.SemaphoreType.DMA
    vmem = pl.BlockSpec(memory_space=pltpu.VMEM)
    return pl.pallas_call(
        gather_and_multiply,
        out_shape=jax.ShapeDtypeStruct((NTAU, ROWS, COLS), jnp.float32),
        in_specs=[vmem, vmem, vmem, vmem, pl.BlockSpec(memory_space=pltpu.SMEM)],
        out_specs=vmem,
        scratch_shapes=[
            pltpu.VMEM((PIECES, BLOCK, WIDTH), jnp.bfloat16),
            pltpu.VMEM((PIECES, ROWS, WIDTH), jnp.bfloat16),
            pltpu.VMEM((PIECES, COLS, WIDTH), jnp.bfloat16),
            pltpu.VMEM((PIECES, NTAU, WIDTH), jnp.float32),
            pltpu.VMEM((NTAU, ROWS, COLS), jnp.float32),
            pltpu.VMEM((NTAU, ROWS, COLS), jnp.float32),
            dma((PIECES,)), dma,
            dma((GROUP,)), dma((GROUP,)),
            dma((4, GROUP)), dma((4, GROUP)),
            dma((4, GROUP)), dma((4, GROUP)),
            dma((2, 4)), dma((2, 4)),
            dma((8,)), dma((8,)),
            dma,
        ],
        compiler_params=pltpu.CompilerParams(
            collective_id=0, has_side_effects=True, vmem_limit_bytes=48 * 2**20
        ),
        cost_estimate=pl.CostEstimate(flops=1610612736, bytes_accessed=2**21, transcendentals=6144),
    )(occ_orbitals, vir_orbitals, occ_energy.reshape(1, -1), vir_energy.reshape(1, -1), tau_points)


def solution(mesh):
    placed = (P(("row", "col"), None), P(("row", "col"), None), P(), P(), P())
    return jax.shard_map(
        local, mesh=mesh, in_specs=placed, out_specs=P(None, "row", "col"), check_vma=False
    )
```

time: 416 us -> 65.7 us (0.16)
  the two profiles are of different devices: /device:TPU:6 before, /device:TPU:1 now
where the time goes in v1:
time: 65.7 us; the launch traced here: 65.4 us
  Pallas kernels  60.7 us (92%)
  local copies, waits for them, and re-layouts  4.61 us (7%)
    pallas_call x1, Pallas kernels, local(): pl.pallas_call(gather_and_multiply, out_shape=jax.ShapeDtypeStruct((NTAU,...  60.7 us
    unnamed x11, local copies, waits for them, and re-layouts  4.61 us

profile of v1, /device:TPU:1, one launch (start us, length us, event | category | flops | bytes accessed | tf_op | source)
XLA Modules:
  0.0 65.4 jit_solution(14696578555162673231)
XLA Ops:
  0.0 0.0 copy-start.4
  0.0 0.7 copy-done.4
  0.7 0.0 copy-start
  0.7 0.8 %copy-done = bf16[16,2048]{1,0:T(8,128)(2,1)S(1)} copy-done((bf16[16,2048]{1,0:T(8,128)(2,1)S(1)}, bf16[16,2048]{1,0:T(8,128)(2,1)}, u32[]{:S(2)}) %copy-start) | copy-done | bytes 65560
  1.5 0.0 copy-start.1
  1.5 0.8 %copy-done.1 = bf16[16,1024]{1,0:T(8,128)(2,1)S(1)} copy-done((bf16[16,1024]{1,0:T(8,128)(2,1)S(1)}, bf16[16,1024]{1,0:T(8,128)(2,1)}, u32[]{:S(2)}) %copy-start.1) | copy-done | bytes 32792
  2.3 0.0 copy-start.2
  2.3 0.7 %copy-done.2 = f32[2048]{0:T(1024)S(1)} copy-done((f32[2048]{0:T(1024)S(1)}, f32[2048]{0:T(1024)}, u32[]{:S(2)}) %copy-start.2) | copy-done | bytes 8216
  3.0 0.0 copy-start.3
  3.0 0.7 %copy-done.3 = f32[1024]{0:T(1024)S(1)} copy-done((f32[1024]{0:T(1024)S(1)}, f32[1024]{0:T(1024)}, u32[]{:S(2)}) %copy-start.3) | copy-done | bytes 4120
  3.6 60.7 %shard_map.55 = f32[2,256,512]{2,1,0:T(8,128)S(1)} custom-call(bf16[16,2048]{1,0:T(8,128)(2,1)S(1)} %copy-done, bf16[16,1024]{1,0:T(8,128)(2,1)S(1)} %copy-done.1, f32[1,2048]{1,0:T(1,128)S(1)} %bitcast.2, f32[1,1024]{1,0:T(1,128)S(1)} %bitcast.3, f32[2]{0:T(128)S(1)} %copy-done.4), custom_call_target="tpu_custom_call" | custom-call | flops 1610612736 | bytes 2097152 | tf_op jit(solution)/shard_map/pallas_call | solution.py:235
  64.4 1.0 %copy.7 = f32[2,256,512]{2,1,0:T(8,128)} copy(f32[2,256,512]{2,1,0:T(8,128)S(1)} %shard_map.55) | data formatting | bytes 2097152
Async XLA Ops:
  0.0 0.7 %copy-start.4 = (f32[2]{0:T(128)S(1)}, f32[2]{0:T(128)}, u32[]{:S(2)}) copy-start(f32[2]{0:T(128)} %tau_ref.1) | copy-start | bytes 28
  0.7 0.8 %copy-start = (bf16[16,2048]{1,0:T(8,128)(2,1)S(1)}, bf16[16,2048]{1,0:T(8,128)(2,1)}, u32[]{:S(2)}) copy-start(bf16[16,2048]{1,0:T(8,128)(2,1)} %occ_ref.1) | copy-start | bytes 196612
  1.5 0.8 %copy-start.1 = (bf16[16,1024]{1,0:T(8,128)(2,1)S(1)}, bf16[16,1024]{1,0:T(8,128)(2,1)}, u32[]{:S(2)}) copy-start(bf16[16,1024]{1,0:T(8,128)(2,1)} %vir_ref.1) | copy-start | bytes 98308
  2.3 0.7 %copy-start.2 = (f32[2048]{0:T(1024)S(1)}, f32[2048]{0:T(1024)}, u32[]{:S(2)}) copy-start(f32[2048]{0:T(1024)} %param.7) | copy-start | bytes 24580
  3.0 0.7 %copy-start.3 = (f32[1024]{0:T(1024)S(1)}, f32[1024]{0:T(1024)}, u32[]{:S(2)}) copy-start(f32[1024]{0:T(1024)} %param.8) | copy-start | bytes 12292

commit v2 on v0

v2 whole, which is shorter than its diff:
```python
import jax
import jax.numpy as jnp
from jax import lax
from jax.experimental import pallas as pl
from jax.experimental.pallas import tpu as pltpu
from jax.sharding import PartitionSpec as P

SLICES = 8
OCC_W = 256
VIR_W = 128
WIDTH = OCC_W + VIR_W
BLOCK = 16
ROWS = 256
COLS = 512
RUN = 4
NTAU = 2
CARRIED = (0, 2, 3)
MESH = pl.DeviceIdType.MESH


def gather_and_multiply(
    occ_hbm, vir_hbm, occ_energy_hbm, vir_energy_hbm, tau_hbm, out_ref,
    occ, vir, occ_energy, vir_energy, tau, own, scattered, lined, rows, cols, scales, total_occ, total_vir,
    in_sem, y_send, y_recv, x_send, x_recv, z_send, z_recv, up_send, up_recv, down_send, down_recv,
    pair_send, pair_recv, row_send, row_recv, core_send, core_recv, own_sem,
):
    row, col = lax.axis_index("row"), lax.axis_index("col")
    y, z_lo = row // RUN, row % RUN
    x, z_hi, core = col // 4, col // 2 % 2, col % 2

    def flip(value, k):
        return (value, value + 1 - 2 * (value % 2), (value + 2) % 4, 3 - value)[k]

    def at_y(steps):
        return ((row + RUN * steps) % (SLICES * RUN), col)

    def at_x(steps):
        return (row, (col + 4 * steps) % 16)

    over = col + 2 - 4 * z_hi
    across = (row, over)
    sibling = (row, col + 1 - 2 * core)
    pair = (y * RUN + flip(z_lo, 1), col)

    part = 2 * z_hi + z_lo % 2

    def spread(half, k):
        return (y * RUN + flip(part, k), 4 * x + 2 * half + z_lo // 2)

    def spread_source(k, source_core):
        chunk_at = flip(z_lo, k)
        return (y * RUN + 2 * core + chunk_at % 2, 4 * x + 2 * (chunk_at // 2) + source_core)

    inputs = [
        pltpu.make_async_copy(src, dst, in_sem.at[i])
        for i, (src, dst) in enumerate((
            (occ_hbm, occ), (vir_hbm, vir), (occ_energy_hbm, occ_energy), (vir_energy_hbm, vir_energy), (tau_hbm, tau),
        ))
    ]
    for copy in inputs:
        copy.start()

    barrier = pltpu.get_barrier_semaphore()
    partners = [at_y(s) for s in (4, 3, 5, 2, 6, 1, 7)] + [across] + [at_x(s) for s in (2, 1, 3)] + [pair, sibling]
    partners += [spread_source(k, c) for k in CARRIED for c in range(2)]
    for place in partners:
        pl.semaphore_signal(barrier, inc=1, device_id=place, device_id_type=MESH)

    inputs[0].wait()
    inputs[1].wait()
    for j in range(SLICES):
        own[j, :, :OCC_W] = occ[:, j * OCC_W:(j + 1) * OCC_W]
        own[j, :, OCC_W:] = vir[:, j * VIR_W:(j + 1) * VIR_W]
    pl.semaphore_wait(barrier, len(partners))

    def remote(src, dst, send, recv, place):
        return pltpu.make_async_remote_copy(
            src_ref=src, dst_ref=dst, send_sem=send, recv_sem=recv, device_id=place, device_id_type=MESH
        )

    sent = []

    def send(*args):
        sent.append(remote(*args))
        sent[-1].start()

    def arrived(ref, sem):
        pltpu.make_async_copy(ref, ref, sem).wait()

    for steps in (1, 7, 2, 6, 3, 5, 4):
        send(own.at[(y + steps) % SLICES], scattered.at[y], y_send.at[steps], y_recv, at_y(steps))
    pltpu.make_async_copy(own.at[y], scattered.at[y], y_recv).start()

    def row_spot(c):
        return rows.at[:, pl.ds(pl.multiple_of(c * BLOCK, BLOCK), BLOCK)]

    send(own, row_spot(col), row_send.at[0, 0], row_recv.at[0, 0], across)
    send(own, row_spot(col), core_send.at[0], core_recv.at[0], sibling)
    own_copy = pltpu.make_async_copy(own, row_spot(col), own_sem)
    own_copy.start()

    for i in range(2, 5):
        inputs[i].wait()
    for j in range(SLICES):
        for t in range(NTAU):
            tau_at = tau[:, t:t + 1]
            scales[j, t:t + 1, :OCC_W] = jnp.exp(tau_at * occ_energy[:, j * OCC_W:(j + 1) * OCC_W])
            scales[j, t:t + 1, OCC_W:] = jnp.exp(-tau_at * vir_energy[:, j * VIR_W:(j + 1) * VIR_W])

    arrived(scattered, y_recv)
    for steps in (1, 3, 2):
        there = (x + steps) % 4
        send(scattered.at[pl.ds(2 * there, 2)], lined.at[:, x], x_send.at[steps], x_recv, at_x(steps))
    pltpu.make_async_copy(scattered.at[pl.ds(2 * x, 2)], lined.at[:, x], x_recv).start()
    for steps in (1, 3, 2):
        send(own, row_spot(col), row_send.at[0, steps], row_recv.at[0, steps], at_x(steps))

    arrived(lined, x_recv)
    spread_copies = []
    for k in CARRIED:
        for half in range(2):
            place = spread(half, k)
            spot = cols.at[y, z_lo % 2, :, z_hi, pl.ds(pl.multiple_of(core * BLOCK, BLOCK), BLOCK)]
            here = jnp.logical_and(place[0] == row, place[1] == col)
            copy = remote(lined.at[half], spot, z_send.at[half, k], z_recv.at[k], place)
            spread_copies.append((here, copy))

            @pl.when(here)
            def _():
                pltpu.make_async_copy(lined.at[half], spot, z_recv.at[k]).start()

            @pl.when(jnp.logical_not(here))
            def _():
                copy.start()

    def chunk(j, k, xs=slice(0, 4)):
        at = flip(z_lo, k)
        return cols.at[j, at % 2, pl.ds(xs.start, xs.stop - xs.start), at // 2]

    whole, first, second = slice(0, 4), slice(0, 2), slice(2, 4)
    last_up = {CARRIED[0]: whole, CARRIED[1]: first}
    last_down = {CARRIED[2]: whole, CARRIED[1]: second}

    def pass_up(step, k, xs=whole):
        ref = chunk((y + SLICES - step) % SLICES, k, xs)
        send(ref, ref, up_send.at[step, k], up_recv.at[step, k], at_y(1))

    def pass_down(step, k, xs=whole):
        ref = chunk((y + step) % SLICES, k, xs)
        send(ref, ref, down_send.at[step, k], down_recv.at[step, k], at_y(7))

    def share(distance, j):
        send(chunk(j, 0), chunk(j, 0), pair_send.at[distance], pair_recv.at[distance], pair)

    def from_spread(k):
        arrived(chunk(y, k), z_recv.at[k])
        pass_up(0, k)
        pass_down(0, k)
        if k == 0:
            share(0, y)

    def from_below(step, k):
        xs = whole if step < 3 else last_up[k]
        j = (y + SLICES - step - 1) % SLICES
        arrived(chunk(j, k, xs), up_recv.at[step, k])
        if step < 2:
            pass_up(step + 1, k)
        elif step == 2 and k in last_up:
            pass_up(3, k, last_up[k])
        if k == 0:
            share(SLICES - step - 1, j)

    def from_above(step, k):
        xs = whole if step < 3 else last_down[k]
        j = (y + step + 1) % SLICES
        arrived(chunk(j, k, xs), down_recv.at[step, k])
        if step < 2:
            pass_down(step + 1, k)
        elif step == 2 and k in last_down:
            pass_down(3, k, last_down[k])
        if k == 0:
            share(step + 1, j)

    contract = (((1,), (1,)), ((), ()))

    def grams(j, t):
        panel = rows[j].astype(jnp.float32)
        weighted = (panel * scales[j, pl.ds(t, 1), :]).astype(jnp.bfloat16)
        columns = cols[j].reshape(COLS, WIDTH)
        gram_occ = lax.dot_general(
            weighted[:, :OCC_W], columns[:, :OCC_W], contract, preferred_element_type=jnp.float32
        )
        gram_vir = lax.dot_general(
            weighted[:, OCC_W:], columns[:, OCC_W:], contract, preferred_element_type=jnp.float32
        )
        return gram_occ, gram_vir

    def accumulate(distance):
        j = (y + distance) % SLICES
        arrived(chunk(j, 1), pair_recv.at[distance])

        @pl.loop(0, NTAU)
        def _(t):
            gram_occ, gram_vir = grams(j, t)
            if distance == 0:
                total_occ[t] = gram_occ
                total_vir[t] = gram_vir
            else:
                total_occ[t] += gram_occ
                total_vir[t] += gram_vir

    def rows_from_across():
        arrived(row_spot(over), row_recv.at[0, 0])
        for steps in (1, 3, 2):
            send(row_spot(over), row_spot(over), row_send.at[1, steps], row_recv.at[1, steps], at_x(steps))
        send(row_spot(over), row_spot(over), core_send.at[1], core_recv.at[1], sibling)

    def rows_from_beside(which):
        for i, steps in enumerate((1, 3, 2)):
            c = ((over if which else col) + 16 - 4 * steps) % 16
            arrived(row_spot(c), row_recv.at[which, steps])
            slot = 2 + 3 * which + i
            send(row_spot(c), row_spot(c), core_send.at[slot], core_recv.at[slot], sibling)

    def rows_complete():
        own_copy.wait()
        for slot in range(8):
            arrived(row_spot(col), core_recv.at[slot])

    events = [(0.0, rows_from_across, ())]
    for i, k in enumerate(CARRIED):
        events.append((2.5 * (i + 1), from_spread, (k,)))
        for step in range(3):
            at = 2.5 * (i + 1) + 4.2 + 6.2 * step
            events += [(at, from_below, (step, k)), (at, from_above, (step, k))]
    events += [(11.0, rows_from_beside, (0,)), (13.0, rows_from_beside, (1,)), (17.0, rows_complete, ())]
    events += [(18.0, accumulate, (0,)), (18.1, accumulate, (1,)), (18.2, accumulate, (7,))]
    events += [(23.0, accumulate, (2,)), (23.1, accumulate, (6,))]
    events += [(40.0, from_below, (3, k)) for k in last_up] + [(41.0, from_above, (3, k)) for k in last_down]
    events += [(42.0, accumulate, (3,)), (42.1, accumulate, (5,))]
    for _, wait_for, args in sorted(events, key=lambda event: event[0]):
        wait_for(*args)

    last = (y + 4) % SLICES
    arrived(chunk(last, 1), pair_recv.at[4])
    for t in range(NTAU):
        gram_occ, gram_vir = grams(last, t)
        out_ref[t] = -((total_occ[t] + gram_occ) * (total_vir[t] + gram_vir))

    for copy in sent:
        copy.wait_send()
    for here, copy in spread_copies:
        @pl.when(jnp.logical_not(here))
        def _():
            copy.wait_send()


def local(occ_orbitals, vir_orbitals, occ_energy, vir_energy, tau_points):
    dma = pltpu.SemaphoreType.DMA
    place = pl.BlockSpec(memory_space=pl.ANY)
    bf16, f32 = jnp.bfloat16, jnp.float32
    return pl.pallas_call(
        gather_and_multiply,
        out_shape=jax.ShapeDtypeStruct((NTAU, ROWS, COLS), f32),
        in_specs=[place] * 5,
        out_specs=pl.BlockSpec(memory_space=pltpu.VMEM),
        scratch_shapes=[
            pltpu.VMEM(occ_orbitals.shape, bf16),
            pltpu.VMEM(vir_orbitals.shape, bf16),
            pltpu.VMEM((1, SLICES * OCC_W), f32),
            pltpu.VMEM((1, SLICES * VIR_W), f32),
            pltpu.VMEM((1, NTAU), f32),
            pltpu.VMEM((SLICES, BLOCK, WIDTH), bf16),
            pltpu.VMEM((SLICES, BLOCK, WIDTH), bf16),
            pltpu.VMEM((2, 4, BLOCK, WIDTH), bf16),
            pltpu.VMEM((SLICES, ROWS, WIDTH), bf16),
            pltpu.VMEM((SLICES, 2, 4, 2, 2 * BLOCK, WIDTH), bf16),
            pltpu.VMEM((SLICES, NTAU, WIDTH), f32),
            pltpu.VMEM((NTAU, ROWS, COLS), f32),
            pltpu.VMEM((NTAU, ROWS, COLS), f32),
            dma((5,)),
            dma((SLICES,)), dma,
            dma((4,)), dma,
            dma((2, 4)), dma((4,)),
            dma((4, 4)), dma((4, 4)),
            dma((4, 4)), dma((4, 4)),
            dma((SLICES,)), dma((SLICES,)),
            dma((2, 4)), dma((2, 4)),
            dma((8,)), dma((8,)),
            dma,
        ],
        compiler_params=pltpu.CompilerParams(
            collective_id=0, has_side_effects=True, vmem_limit_bytes=56 * 2**20
        ),
        cost_estimate=pl.CostEstimate(flops=1610612736, bytes_accessed=2**21, transcendentals=6144),
    )(occ_orbitals, vir_orbitals, occ_energy.reshape(1, -1), vir_energy.reshape(1, -1), tau_points.reshape(1, -1))


def solution(mesh):
    placed = (P(("row", "col"), None), P(("row", "col"), None), P(), P(), P())
    return jax.shard_map(
        local, mesh=mesh, in_specs=placed, out_specs=P(None, "row", "col"), check_vma=False
    )
```

time: 416 us -> 60.6 us (0.15)
  the two profiles are of different devices: /device:TPU:6 before, /device:TPU:1 now
where the time goes in v2:
time: 60.6 us; the launch traced here: 60.4 us
  Pallas kernels  58.1 us (96%)
  local copies, waits for them, and re-layouts  2.26 us (4%)
    pallas_call x1, Pallas kernels, local(): pl.pallas_call(gather_and_multiply, out_shape=jax.ShapeDtypeStruct((NTAU,...  58.1 us
    unnamed x1, local copies, waits for them, and re-layouts  2.26 us

profile of v2, /device:TPU:1, one launch (start us, length us, event | category | flops | bytes accessed | tf_op | source)
XLA Modules:
  0.0 60.4 jit_solution(2734052516887517838)
XLA Ops:
  0.0 58.1 %shard_map.55 = f32[2,256,512]{2,1,0:T(8,128)} custom-call(bf16[16,2048]{1,0:T(8,128)(2,1)} %occ_hbm.1, bf16[16,1024]{1,0:T(8,128)(2,1)} %vir_hbm.1, f32[1,2048]{1,0:T(1,128)} %bitcast.3, f32[1,1024]{1,0:T(1,128)} %bitcast.4, f32[1,2]{1,0:T(1,128)} %bitcast.5), custom_call_target="tpu_custom_call" | custom-call | flops 1610612736 | bytes 2097152 | tf_op jit(solution)/shard_map/pallas_call | solution.py:262
  58.1 2.3 %copy.7 = f32[2,256,512]{2,1,0:T(8,128)} copy(f32[2,256,512]{2,1,0:T(8,128)} %shard_map.55) | data formatting | bytes 2097152

commit v3 on v2

--- a/solution.py
+++ b/solution.py
@@ -14,7 +14,6 @@
 COLS = 512
 RUN = 4
 NTAU = 2
-CARRIED = (0, 2, 3)
 MESH = pl.DeviceIdType.MESH
 
 
@@ -22,15 +21,12 @@
     occ_hbm, vir_hbm, occ_energy_hbm, vir_energy_hbm, tau_hbm, out_ref,
     occ, vir, occ_energy, vir_energy, tau, own, scattered, lined, rows, cols, scales, total_occ, total_vir,
     in_sem, y_send, y_recv, x_send, x_recv, z_send, z_recv, up_send, up_recv, down_send, down_recv,
-    pair_send, pair_recv, row_send, row_recv, core_send, core_recv, own_sem,
+    pair_send, pair_recv, row_send, row_recv, core_send, core_recv, own_sem, go,
 ):
     row, col = lax.axis_index("row"), lax.axis_index("col")
     y, z_lo = row // RUN, row % RUN
     x, z_hi, core = col // 4, col // 2 % 2, col % 2
 
-    def flip(value, k):
-        return (value, value + 1 - 2 * (value % 2), (value + 2) % 4, 3 - value)[k]
-
     def at_y(steps):
         return ((row + RUN * steps) % (SLICES * RUN), col)
 
@@ -40,16 +36,20 @@
     over = col + 2 - 4 * z_hi
     across = (row, over)
     sibling = (row, col + 1 - 2 * core)
-    pair = (y * RUN + flip(z_lo, 1), col)
-
-    part = 2 * z_hi + z_lo % 2
-
-    def spread(half, k):
-        return (y * RUN + flip(part, k), 4 * x + 2 * half + z_lo // 2)
-
-    def spread_source(k, source_core):
-        chunk_at = flip(z_lo, k)
-        return (y * RUN + 2 * core + chunk_at % 2, 4 * x + 2 * (chunk_at // 2) + source_core)
+    pair = (y * RUN + z_lo + 1 - 2 * (z_lo % 2), col)
+
+    parity, owner = z_lo % 2, z_lo // 2
+
+    def spread(half, to):
+        return (y * RUN + to, 4 * x + 2 * half + owner)
+
+    def early_source(source_core):
+        return (y * RUN + 2 * core + parity, 4 * x + source_core)
+
+    def late_source(p, source_core):
+        return (y * RUN + 2 * core + p, 4 * x + 2 + source_core)
+
+    early, late = z_hi == 0, z_hi == 1
 
     inputs = [
         pltpu.make_async_copy(src, dst, in_sem.at[i])
@@ -61,17 +61,35 @@
         copy.start()
 
     barrier = pltpu.get_barrier_semaphore()
-    partners = [at_y(s) for s in (4, 3, 5, 2, 6, 1, 7)] + [across] + [at_x(s) for s in (2, 1, 3)] + [pair, sibling]
-    partners += [spread_source(k, c) for k in CARRIED for c in range(2)]
-    for place in partners:
-        pl.semaphore_signal(barrier, inc=1, device_id=place, device_id_type=MESH)
+    lates = [late_source(p, c) for p in range(2) for c in range(2)]
+    earlies = [early_source(c) for c in range(2)]
+    partners = [at_y(s) for s in (4, 3, 5, 2, 6, 1, 7)] + [at_x(s) for s in (2, 1, 3)] + [pair, sibling]
+
+    def signal(semaphore, places):
+        for place in places:
+            pl.semaphore_signal(semaphore, inc=1, device_id=place, device_id_type=MESH)
+
+    signal(barrier, partners)
+
+    @pl.when(early)
+    def _():
+        signal(barrier, [across] + lates + earlies + [spread(1, parity + 2 * i) for i in range(2)])
+
+    @pl.when(late)
+    def _():
+        signal(barrier, lates)
 
     inputs[0].wait()
     inputs[1].wait()
     for j in range(SLICES):
         own[j, :, :OCC_W] = occ[:, j * OCC_W:(j + 1) * OCC_W]
         own[j, :, OCC_W:] = vir[:, j * VIR_W:(j + 1) * VIR_W]
-    pl.semaphore_wait(barrier, len(partners))
+    pl.semaphore_wait(barrier, len(partners) + 2 + 9 * z_hi)
+
+    @pl.when(late)
+    def _():
+        signal(go, [across] + earlies)
+
 
     def remote(src, dst, send, recv, place):
         return pltpu.make_async_remote_copy(
@@ -80,9 +98,12 @@
 
     sent = []
 
+    def launch(build, *args):
+        sent.append((build, args))
+        build(*args).start()
+
     def send(*args):
-        sent.append(remote(*args))
-        sent[-1].start()
+        launch(remote, *args)
 
     def arrived(ref, sem):
         pltpu.make_async_copy(ref, ref, sem).wait()
@@ -94,7 +115,13 @@
     def row_spot(c):
         return rows.at[:, pl.ds(pl.multiple_of(c * BLOCK, BLOCK), BLOCK)]
 
-    send(own, row_spot(col), row_send.at[0, 0], row_recv.at[0, 0], across)
+    row_across = remote(own, row_spot(col), row_send.at[0, 0], row_recv.at[0, 0], across)
+    sent.append((lambda: row_across, ()))
+
+    @pl.when(late)
+    def _():
+        row_across.start()
+
     send(own, row_spot(col), core_send.at[0], core_recv.at[0], sibling)
     own_copy = pltpu.make_async_copy(own, row_spot(col), own_sem)
     own_copy.start()
@@ -112,52 +139,80 @@
         there = (x + steps) % 4
         send(scattered.at[pl.ds(2 * there, 2)], lined.at[:, x], x_send.at[steps], x_recv, at_x(steps))
     pltpu.make_async_copy(scattered.at[pl.ds(2 * x, 2)], lined.at[:, x], x_recv).start()
-    for steps in (1, 3, 2):
-        send(own, row_spot(col), row_send.at[0, steps], row_recv.at[0, steps], at_x(steps))
 
     arrived(lined, x_recv)
     spread_copies = []
-    for k in CARRIED:
+
+    def spread_out(kind, half, to, active, slot):
+        place = spread(half, to)
+        spot = cols.at[y, parity, :, z_hi, pl.ds(pl.multiple_of(core * BLOCK, BLOCK), BLOCK)]
+        here = jnp.logical_and(place[0] == row, place[1] == col)
+        copy = remote(lined.at[half], spot, z_send.at[slot], z_recv.at[kind], place)
+        there = jnp.logical_and(active, jnp.logical_not(here))
+        spread_copies.append((there, copy))
+
+        @pl.when(jnp.logical_and(active, here))
+        def _():
+            pltpu.make_async_copy(lined.at[half], spot, z_recv.at[kind]).start()
+
+        @pl.when(there)
+        def _():
+            copy.start()
+
+    for i in range(2):
+        spread_out(0, 0, parity + 2 * i, early, i)
+    for to in range(RUN):
         for half in range(2):
-            place = spread(half, k)
-            spot = cols.at[y, z_lo % 2, :, z_hi, pl.ds(pl.multiple_of(core * BLOCK, BLOCK), BLOCK)]
-            here = jnp.logical_and(place[0] == row, place[1] == col)
-            copy = remote(lined.at[half], spot, z_send.at[half, k], z_recv.at[k], place)
-            spread_copies.append((here, copy))
-
-            @pl.when(here)
-            def _():
-                pltpu.make_async_copy(lined.at[half], spot, z_recv.at[k]).start()
-
-            @pl.when(jnp.logical_not(here))
-            def _():
-                copy.start()
-
-    def chunk(j, k, xs=slice(0, 4)):
-        at = flip(z_lo, k)
-        return cols.at[j, at % 2, pl.ds(xs.start, xs.stop - xs.start), at // 2]
+            spread_out(1 + parity, half, to, late, 4 + 2 * to + half)
+
+    def to_late_half():
+        @pl.when(early)
+        def _():
+            pl.semaphore_wait(go, 3)
+
+        for i in range(2):
+            spread_out(0, 1, parity + 2 * i, early, 2 + i)
+
+    def early_row_across():
+        @pl.when(early)
+        def _():
+            row_across.start()
+
+    def chunk(j, kind, xs=slice(0, 4)):
+        p = (parity, 0, 1, 1 - parity)[kind]
+        return cols.at[j, p, pl.ds(xs.start, xs.stop - xs.start), (0, 1, 1, 0)[kind]]
 
     whole, first, second = slice(0, 4), slice(0, 2), slice(2, 4)
-    last_up = {CARRIED[0]: whole, CARRIED[1]: first}
-    last_down = {CARRIED[2]: whole, CARRIED[1]: second}
+    last_up = {0: first, 1: whole}
+    last_down = {0: second, 2: whole}
+
+    def up_copy(step, k, xs):
+        ref = chunk((y + SLICES - step) % SLICES, k, xs)
+        return remote(ref, ref, up_send.at[step, k], up_recv.at[step, k], at_y(1))
+
+    def down_copy(step, k, xs):
+        ref = chunk((y + step) % SLICES, k, xs)
+        return remote(ref, ref, down_send.at[step, k], down_recv.at[step, k], at_y(7))
+
+    def pair_copy(slot, xs):
+        ref = chunk((y + (4 if slot == 8 else slot)) % SLICES, 0, xs)
+        return remote(ref, ref, pair_send.at[slot], pair_recv.at[slot], pair)
 
     def pass_up(step, k, xs=whole):
-        ref = chunk((y + SLICES - step) % SLICES, k, xs)
-        send(ref, ref, up_send.at[step, k], up_recv.at[step, k], at_y(1))
+        launch(up_copy, step, k, xs)
 
     def pass_down(step, k, xs=whole):
-        ref = chunk((y + step) % SLICES, k, xs)
-        send(ref, ref, down_send.at[step, k], down_recv.at[step, k], at_y(7))
-
-    def share(distance, j):
-        send(chunk(j, 0), chunk(j, 0), pair_send.at[distance], pair_recv.at[distance], pair)
+        launch(down_copy, step, k, xs)
+
+    def share(slot, xs=whole):
+        launch(pair_copy, slot, xs)
 
     def from_spread(k):
         arrived(chunk(y, k), z_recv.at[k])
         pass_up(0, k)
         pass_down(0, k)
         if k == 0:
-            share(0, y)
+            share(0)
 
     def from_below(step, k):
         xs = whole if step < 3 else last_up[k]
@@ -168,7 +223,7 @@
         elif step == 2 and k in last_up:
             pass_up(3, k, last_up[k])
         if k == 0:
-            share(SLICES - step - 1, j)
+            share(SLICES - step - 1, xs)
 
     def from_above(step, k):
         xs = whole if step < 3 else last_down[k]
@@ -179,7 +234,21 @@
         elif step == 2 and k in last_down:
             pass_down(3, k, last_down[k])
         if k == 0:
-            share(step + 1, j)
+            share(step + 1 if step < 3 else 8, xs)
+
+    def from_both(step, k):
+        from_below(step, k)
+        from_above(step, k)
+
+    def only(half, step, k):
+        count = len(sent)
+
+        @pl.when(half)
+        def _():
+            from_both(step, k)
+        again = sent[count:]
+        del sent[count:]
+        return again
 
     contract = (((1,), (1,)), ((), ()))
 
@@ -197,7 +266,7 @@
 
     def accumulate(distance):
         j = (y + distance) % SLICES
-        arrived(chunk(j, 1), pair_recv.at[distance])
+        arrived(chunk(j, 3), pair_recv.at[distance])
 
         @pl.loop(0, NTAU)
         def _(t):
@@ -227,30 +296,47 @@
         for slot in range(8):
             arrived(row_spot(col), core_recv.at[slot])
 
-    events = [(0.0, rows_from_across, ())]
-    for i, k in enumerate(CARRIED):
-        events.append((2.5 * (i + 1), from_spread, (k,)))
-        for step in range(3):
-            at = 2.5 * (i + 1) + 4.2 + 6.2 * step
-            events += [(at, from_below, (step, k)), (at, from_above, (step, k))]
-    events += [(11.0, rows_from_beside, (0,)), (13.0, rows_from_beside, (1,)), (17.0, rows_complete, ())]
-    events += [(18.0, accumulate, (0,)), (18.1, accumulate, (1,)), (18.2, accumulate, (7,))]
-    events += [(23.0, accumulate, (2,)), (23.1, accumulate, (6,))]
-    events += [(40.0, from_below, (3, k)) for k in last_up] + [(41.0, from_above, (3, k)) for k in last_down]
-    events += [(42.0, accumulate, (3,)), (42.1, accumulate, (5,))]
-    for _, wait_for, args in sorted(events, key=lambda event: event[0]):
-        wait_for(*args)
+    to_late_half()
+    from_spread(0)
+    from_both(0, 0)
+    early_row_across()
+    sent += only(early, 1, 0)
+    from_spread(1)
+    for steps in (1, 3, 2):
+        send(own, row_spot(col), row_send.at[0, steps], row_recv.at[0, steps], at_x(steps))
+    from_spread(2)
+    rows_from_across()
+    sent += only(early, 2, 0)
+    only(late, 1, 0)
+    rows_from_beside(0)
+    from_both(0, 1)
+    from_both(0, 2)
+    only(late, 2, 0)
+    rows_from_beside(1)
+    from_both(1, 1)
+    from_both(1, 2)
+    rows_complete()
+    for distance in (0, 1, 7):
+        accumulate(distance)
+    from_both(3, 0)
+    from_both(2, 1)
+    from_both(2, 2)
+    for distance in (2, 6, 3, 5):
+        accumulate(distance)
+    from_below(3, 1)
+    from_above(3, 2)
 
     last = (y + 4) % SLICES
-    arrived(chunk(last, 1), pair_recv.at[4])
+    arrived(chunk(last, 3, first), pair_recv.at[4])
+    arrived(chunk(last, 3, second), pair_recv.at[8])
     for t in range(NTAU):
         gram_occ, gram_vir = grams(last, t)
         out_ref[t] = -((total_occ[t] + gram_occ) * (total_vir[t] + gram_vir))
 
-    for copy in sent:
-        copy.wait_send()
-    for here, copy in spread_copies:
-        @pl.when(jnp.logical_not(here))
+    for build, args in sent:
+        build(*args).wait_send()
+    for there, copy in spread_copies:
+        @pl.when(there)
         def _():
             copy.wait_send()
 
@@ -281,13 +367,14 @@
             dma((5,)),
             dma((SLICES,)), dma,
             dma((4,)), dma,
-            dma((2, 4)), dma((4,)),
-            dma((4, 4)), dma((4, 4)),
-            dma((4, 4)), dma((4, 4)),
-            dma((SLICES,)), dma((SLICES,)),
+            dma((12,)), dma((3,)),
+            dma((4, 3)), dma((4, 3)),
+            dma((4, 3)), dma((4, 3)),
+            dma((SLICES + 1,)), dma((SLICES + 1,)),
             dma((2, 4)), dma((2, 4)),
             dma((8,)), dma((8,)),
             dma,
+            pltpu.SemaphoreType.REGULAR,
         ],
         compiler_params=pltpu.CompilerParams(
             collective_id=0, has_side_effects=True, vmem_limit_bytes=56 * 2**20

time: 60.6 us -> 57.1 us (0.942)
  Pallas kernels: 58.1 us -> 54.6 us
    pallas_call x1, Pallas kernels: 58.1 us -> 54.6 us  [local(): pl.pallas_call(gather_and_multiply, out_shape=jax.ShapeDtypeStruct((NTAU,...]
where the time goes in v3:
time: 57.1 us; the launch traced here: 56.9 us
  Pallas kernels  54.6 us (96%)
  local copies, waits for them, and re-layouts  2.26 us (4%)
    pallas_call x1, Pallas kernels, local(): pl.pallas_call(gather_and_multiply, out_shape=jax.ShapeDtypeStruct((NTAU,...  54.6 us
    unnamed x1, local copies, waits for them, and re-layouts  2.26 us

profile of v3, /device:TPU:1, one launch (start us, length us, event | category | flops | bytes accessed | tf_op | source)
XLA Modules:
  0.0 56.9 jit_solution(11500062408837325249)
XLA Ops:
  0.0 54.6 %shard_map.55 = f32[2,256,512]{2,1,0:T(8,128)} custom-call(bf16[16,2048]{1,0:T(8,128)(2,1)} %occ_hbm.1, bf16[16,1024]{1,0:T(8,128)(2,1)} %vir_hbm.1, f32[1,2048]{1,0:T(1,128)} %bitcast.3, f32[1,1024]{1,0:T(1,128)} %bitcast.4, f32[1,2]{1,0:T(1,128)} %bitcast.5), custom_call_target="tpu_custom_call" | custom-call | flops 1610612736 | bytes 2097152 | tf_op jit(solution)/shard_map/pallas_call | solution.py:348
  54.6 2.3 %copy.7 = f32[2,256,512]{2,1,0:T(8,128)} copy(f32[2,256,512]{2,1,0:T(8,128)} %shard_map.55) | data formatting | bytes 2097152

commit v4 on v3

--- a/solution.py
+++ b/solution.py
@@ -345,6 +345,7 @@
     dma = pltpu.SemaphoreType.DMA
     place = pl.BlockSpec(memory_space=pl.ANY)
     bf16, f32 = jnp.bfloat16, jnp.float32
+    operands = (occ_orbitals, vir_orbitals, occ_energy.reshape(1, -1), vir_energy.reshape(1, -1), tau_points.reshape(1, -1))
     return pl.pallas_call(
         gather_and_multiply,
         out_shape=jax.ShapeDtypeStruct((NTAU, ROWS, COLS), f32),
@@ -377,10 +378,10 @@
             pltpu.SemaphoreType.REGULAR,
         ],
         compiler_params=pltpu.CompilerParams(
-            collective_id=0, has_side_effects=True, vmem_limit_bytes=56 * 2**20
+            collective_id=0, has_side_effects=True, vmem_limit_bytes=40 * 2**20
         ),
         cost_estimate=pl.CostEstimate(flops=1610612736, bytes_accessed=2**21, transcendentals=6144),
-    )(occ_orbitals, vir_orbitals, occ_energy.reshape(1, -1), vir_energy.reshape(1, -1), tau_points.reshape(1, -1))
+    )(*[pltpu.with_memory_space_constraint(operand, pltpu.HBM) for operand in operands])
 
 
 def solution(mesh):

time: 57.1 us -> 54.8 us (0.960)
  local copies, waits for them, and re-layouts: 2.26 us -> 0.97 us
  Pallas kernels: 54.6 us -> 53.6 us
    unnamed x1, local copies, waits for them, and re-layouts: 2.26 us -> 0.97 us
    pallas_call x1, Pallas kernels: 54.6 us -> 53.6 us  [local(): pl.pallas_call(gather_and_multiply, out_shape=jax.ShapeDtypeStruct((NTAU,...]
where the time goes in v4:
time: 54.8 us; the launch traced here: 54.6 us
  Pallas kernels  53.6 us (98%)
  local copies, waits for them, and re-layouts  0.97 us (2%)
    pallas_call x1, Pallas kernels, local(): pl.pallas_call(gather_and_multiply, out_shape=jax.ShapeDtypeStruct((NTAU,...  53.6 us

profile of v4, /device:TPU:1, one launch (start us, length us, event | category | flops | bytes accessed | tf_op | source)
XLA Modules:
  0.0 54.6 jit_solution(2011406317837195768)
XLA Ops:
  0.0 53.6 %shard_map.55 = f32[2,256,512]{2,1,0:T(8,128)S(1)} custom-call(bf16[16,2048]{1,0:T(8,128)(2,1)} %occ_hbm.1, bf16[16,1024]{1,0:T(8,128)(2,1)} %vir_hbm.1, f32[1,2048]{1,0:T(1,128)} %bitcast.3, f32[1,1024]{1,0:T(1,128)} %bitcast.4, f32[1,2]{1,0:T(1,128)} %bitcast.5), custom_call_target="tpu_custom_call" | custom-call | flops 1610612736 | bytes 2097152 | tf_op jit(solution)/shard_map/pallas_call | solution.py:349
  53.6 1.0 %copy.7 = f32[2,256,512]{2,1,0:T(8,128)} copy(f32[2,256,512]{2,1,0:T(8,128)S(1)} %shard_map.55) | data formatting | bytes 2097152

commit v5 on v4

--- a/solution.py
+++ b/solution.py
@@ -21,7 +21,7 @@
     occ_hbm, vir_hbm, occ_energy_hbm, vir_energy_hbm, tau_hbm, out_ref,
     occ, vir, occ_energy, vir_energy, tau, own, scattered, lined, rows, cols, scales, total_occ, total_vir,
     in_sem, y_send, y_recv, x_send, x_recv, z_send, z_recv, up_send, up_recv, down_send, down_recv,
-    pair_send, pair_recv, row_send, row_recv, core_send, core_recv, own_sem, go,
+    pair_send, pair_recv, row_send, row_recv, core_send, core_recv, own_sem, go, straight_send,
 ):
     row, col = lax.axis_index("row"), lax.axis_index("col")
     y, z_lo = row // RUN, row % RUN
@@ -71,9 +71,16 @@
 
     signal(barrier, partners)
 
+    straight = jnp.logical_and(late, y % 2 == 0)
+    scatters = jnp.logical_or(early, y % 2 == 1)
+
+    def straight_place(j, to):
+        return (j * RUN + to, 4 * (y // 2) + owner)
+
     @pl.when(early)
     def _():
-        signal(barrier, [across] + lates + earlies + [spread(1, parity + 2 * i) for i in range(2)])
+        signal(barrier, [across] + earlies + [spread(1, parity + 2 * i) for i in range(2)])
+        signal(barrier, [(2 * x * RUN + 2 * core + p, 4 * there + 2 + c) for p in range(2) for there in range(4) for c in range(2)])
 
     @pl.when(late)
     def _():
@@ -84,7 +91,7 @@
     for j in range(SLICES):
         own[j, :, :OCC_W] = occ[:, j * OCC_W:(j + 1) * OCC_W]
         own[j, :, OCC_W:] = vir[:, j * VIR_W:(j + 1) * VIR_W]
-    pl.semaphore_wait(barrier, len(partners) + 2 + 9 * z_hi)
+    pl.semaphore_wait(barrier, len(partners) + 2 + 5 * z_hi + 32 * z_hi * (1 - y % 2))
 
     @pl.when(late)
     def _():
@@ -108,9 +115,26 @@
     def arrived(ref, sem):
         pltpu.make_async_copy(ref, ref, sem).wait()
 
-    for steps in (1, 7, 2, 6, 3, 5, 4):
-        send(own.at[(y + steps) % SLICES], scattered.at[y], y_send.at[steps], y_recv, at_y(steps))
-    pltpu.make_async_copy(own.at[y], scattered.at[y], y_recv).start()
+    def scatter_copy(steps):
+        return remote(own.at[(y + steps) % SLICES], scattered.at[y], y_send.at[steps], y_recv, at_y(steps))
+
+    around = (1, 7, 2, 6, 3, 5, 4)
+
+    @pl.when(scatters)
+    def _():
+        for steps in around:
+            scatter_copy(steps).start()
+        pltpu.make_async_copy(own.at[y], scattered.at[y], y_recv).start()
+
+    def straight_copy(j, to):
+        spot = cols.at[j, parity, x, 1, pl.ds(pl.multiple_of(core * BLOCK, BLOCK), BLOCK)]
+        return remote(own.at[j], spot, straight_send.at[j, to], z_recv.at[1 + parity], straight_place(j, to))
+
+    @pl.when(straight)
+    def _():
+        for to in (0, 3, 1, 2):
+            for j in range(SLICES):
+                straight_copy(j, to).start()
 
     def row_spot(c):
         return rows.at[:, pl.ds(pl.multiple_of(c * BLOCK, BLOCK), BLOCK)]
@@ -134,13 +158,36 @@
             scales[j, t:t + 1, :OCC_W] = jnp.exp(tau_at * occ_energy[:, j * OCC_W:(j + 1) * OCC_W])
             scales[j, t:t + 1, OCC_W:] = jnp.exp(-tau_at * vir_energy[:, j * VIR_W:(j + 1) * VIR_W])
 
-    arrived(scattered, y_recv)
-    for steps in (1, 3, 2):
+    def pair_of_planes(steps):
         there = (x + steps) % 4
-        send(scattered.at[pl.ds(2 * there, 2)], lined.at[:, x], x_send.at[steps], x_recv, at_x(steps))
-    pltpu.make_async_copy(scattered.at[pl.ds(2 * x, 2)], lined.at[:, x], x_recv).start()
-
-    arrived(lined, x_recv)
+        return scattered.at[pl.ds(2 * there, 2)], lined.at[:, x]
+
+    def odd_plane(steps):
+        there = (x + steps) % 4
+        return scattered.at[2 * there + 1], lined.at[1, x]
+
+    def exchange_copy(parts, steps):
+        src, dst = parts(steps)
+        return remote(src, dst, x_send.at[steps], x_recv, at_x(steps))
+
+    def exchange(parts):
+        for steps in (1, 3, 2):
+            exchange_copy(parts, steps).start()
+        src, dst = parts(0)
+        pltpu.make_async_copy(src, dst, x_recv).start()
+
+    @pl.when(early)
+    def _():
+        arrived(scattered, y_recv)
+        exchange(pair_of_planes)
+        arrived(lined, x_recv)
+
+    @pl.when(late)
+    def _():
+        arrived(scattered.at[pl.ds(0, 4)], y_recv)
+        exchange(odd_plane)
+        arrived(lined.at[0], x_recv)
+
     spread_copies = []
 
     def spread_out(kind, half, to, active, slot):
@@ -162,8 +209,7 @@
     for i in range(2):
         spread_out(0, 0, parity + 2 * i, early, i)
     for to in range(RUN):
-        for half in range(2):
-            spread_out(1 + parity, half, to, late, 4 + 2 * to + half)
+        spread_out(1 + parity, 1, to, late, 4 + 2 * to + 1)
 
     def to_late_half():
         @pl.when(early)
@@ -204,8 +250,19 @@
     def pass_down(step, k, xs=whole):
         launch(down_copy, step, k, xs)
 
+    at_once = (z_lo % 3 == 0) == late
+
     def share(slot, xs=whole):
-        launch(pair_copy, slot, xs)
+        @pl.when(at_once)
+        def _():
+            pair_copy(slot, xs).start()
+
+    def share_later(slot, xs=whole):
+        sent.append((pair_copy, (slot, xs)))
+
+        @pl.when(jnp.logical_not(at_once))
+        def _():
+            pair_copy(slot, xs).start()
 
     def from_spread(k):
         arrived(chunk(y, k), z_recv.at[k])
@@ -305,13 +362,19 @@
     for steps in (1, 3, 2):
         send(own, row_spot(col), row_send.at[0, steps], row_recv.at[0, steps], at_x(steps))
     from_spread(2)
+    for slot in (0, 1, 7):
+        share_later(slot)
     rows_from_across()
     sent += only(early, 2, 0)
     only(late, 1, 0)
+    share_later(2)
+    share_later(6)
     rows_from_beside(0)
     from_both(0, 1)
     from_both(0, 2)
     only(late, 2, 0)
+    share_later(3)
+    share_later(5)
     rows_from_beside(1)
     from_both(1, 1)
     from_both(1, 2)
@@ -319,6 +382,8 @@
     for distance in (0, 1, 7):
         accumulate(distance)
     from_both(3, 0)
+    share_later(4, first)
+    share_later(8, second)
     from_both(2, 1)
     from_both(2, 2)
     for distance in (2, 6, 3, 5):
@@ -335,6 +400,26 @@
 
     for build, args in sent:
         build(*args).wait_send()
+    @pl.when(scatters)
+    def _():
+        for steps in around:
+            scatter_copy(steps).wait_send()
+
+    @pl.when(straight)
+    def _():
+        for j in range(SLICES):
+            for to in range(RUN):
+                straight_copy(j, to).wait_send()
+
+    for steps in (1, 3, 2):
+        @pl.when(early)
+        def _():
+            exchange_copy(pair_of_planes, steps).wait_send()
+
+        @pl.when(late)
+        def _():
+            exchange_copy(odd_plane, steps).wait_send()
+
     for there, copy in spread_copies:
         @pl.when(there)
         def _():
@@ -376,6 +461,7 @@
             dma((8,)), dma((8,)),
             dma,
             pltpu.SemaphoreType.REGULAR,
+            dma((SLICES, RUN)),
         ],
         compiler_params=pltpu.CompilerParams(
             collective_id=0, has_side_effects=True, vmem_limit_bytes=40 * 2**20

time: 54.8 us -> 53.8 us (0.982)
  Pallas kernels: 53.6 us -> 52.6 us
    pallas_call x1, Pallas kernels: 53.6 us -> 52.6 us  [local(): pl.pallas_call(gather_and_multiply, out_shape=jax.ShapeDtypeStruct((NTAU,...]
where the time goes in v5:
time: 53.8 us; the launch traced here: 53.6 us
  Pallas kernels  52.6 us (98%)
  local copies, waits for them, and re-layouts  0.97 us (2%)
    pallas_call x1, Pallas kernels, local(): pl.pallas_call(gather_and_multiply, out_shape=jax.ShapeDtypeStruct((NTAU,...  52.6 us

profile of v5, /device:TPU:1, one launch (start us, length us, event | category | flops | bytes accessed | tf_op | source)
XLA Modules:
  0.0 53.6 jit_solution(15598620464196107398)
XLA Ops:
  0.0 52.6 %shard_map.55 = f32[2,256,512]{2,1,0:T(8,128)S(1)} custom-call(bf16[16,2048]{1,0:T(8,128)(2,1)} %occ_hbm.1, bf16[16,1024]{1,0:T(8,128)(2,1)} %vir_hbm.1, f32[1,2048]{1,0:T(1,128)} %bitcast.3, f32[1,1024]{1,0:T(1,128)} %bitcast.4, f32[1,2]{1,0:T(1,128)} %bitcast.5), custom_call_target="tpu_custom_call" | custom-call | flops 1610612736 | bytes 2097152 | tf_op jit(solution)/shard_map/pallas_call | solution.py:434
  52.6 1.0 %copy.7 = f32[2,256,512]{2,1,0:T(8,128)} copy(f32[2,256,512]{2,1,0:T(8,128)S(1)} %shard_map.55) | data formatting | bytes 2097152

commit v6 on v5

--- a/solution.py
+++ b/solution.py
@@ -118,7 +118,7 @@
     def scatter_copy(steps):
         return remote(own.at[(y + steps) % SLICES], scattered.at[y], y_send.at[steps], y_recv, at_y(steps))
 
-    around = (1, 7, 2, 6, 3, 5, 4)
+    around = (4, 3, 5, 2, 6, 1, 7)
 
     @pl.when(scatters)
     def _():
@@ -250,7 +250,7 @@
     def pass_down(step, k, xs=whole):
         launch(down_copy, step, k, xs)
 
-    at_once = (z_lo % 3 == 0) == late
+    at_once = jnp.logical_or(late, z_lo % 3 != 0)
 
     def share(slot, xs=whole):
         @pl.when(at_once)

time: 53.8 us -> 54 us (level)
  no operation moved by 1% of the time
where the time goes in v6:
time: 54 us; the launch traced here: 53.8 us
  Pallas kernels  52.8 us (98%)
  local copies, waits for them, and re-layouts  0.97 us (2%)
    pallas_call x1, Pallas kernels, local(): pl.pallas_call(gather_and_multiply, out_shape=jax.ShapeDtypeStruct((NTAU,...  52.8 us

profile of v6, /device:TPU:1, one launch (start us, length us, event | category | flops | bytes accessed | tf_op | source)
XLA Modules:
  0.0 53.8 jit_solution(9825635859975820982)
XLA Ops:
  0.0 52.8 %shard_map.55 = f32[2,256,512]{2,1,0:T(8,128)S(1)} custom-call(bf16[16,2048]{1,0:T(8,128)(2,1)} %occ_hbm.1, bf16[16,1024]{1,0:T(8,128)(2,1)} %vir_hbm.1, f32[1,2048]{1,0:T(1,128)} %bitcast.3, f32[1,1024]{1,0:T(1,128)} %bitcast.4, f32[1,2]{1,0:T(1,128)} %bitcast.5), custom_call_target="tpu_custom_call" | custom-call | flops 1610612736 | bytes 2097152 | tf_op jit(solution)/shard_map/pallas_call | solution.py:434
  52.8 1.0 %copy.7 = f32[2,256,512]{2,1,0:T(8,128)} copy(f32[2,256,512]{2,1,0:T(8,128)S(1)} %shard_map.55) | data formatting | bytes 2097152

commit v7 on v5

--- a/solution.py
+++ b/solution.py
@@ -21,7 +21,7 @@
     occ_hbm, vir_hbm, occ_energy_hbm, vir_energy_hbm, tau_hbm, out_ref,
     occ, vir, occ_energy, vir_energy, tau, own, scattered, lined, rows, cols, scales, total_occ, total_vir,
     in_sem, y_send, y_recv, x_send, x_recv, z_send, z_recv, up_send, up_recv, down_send, down_recv,
-    pair_send, pair_recv, row_send, row_recv, core_send, core_recv, own_sem, go, straight_send,
+    pair_send, pair_recv, row_send, row_recv, core_send, core_recv, own_sem, go, straight_send, weighted_last,
 ):
     row, col = lax.axis_index("row"), lax.axis_index("col")
     y, z_lo = row // RUN, row % RUN
@@ -309,9 +309,12 @@
 
     contract = (((1,), (1,)), ((), ()))
 
-    def grams(j, t):
+    def weigh(j, t):
         panel = rows[j].astype(jnp.float32)
-        weighted = (panel * scales[j, pl.ds(t, 1), :]).astype(jnp.bfloat16)
+        return (panel * scales[j, pl.ds(t, 1), :]).astype(jnp.bfloat16)
+
+    def grams(j, t, weighted=None):
+        weighted = weigh(j, t) if weighted is None else weighted
         columns = cols[j].reshape(COLS, WIDTH)
         gram_occ = lax.dot_general(
             weighted[:, :OCC_W], columns[:, :OCC_W], contract, preferred_element_type=jnp.float32
@@ -388,14 +391,15 @@
     from_both(2, 2)
     for distance in (2, 6, 3, 5):
         accumulate(distance)
+    last = (y + 4) % SLICES
+    for t in range(NTAU):
+        weighted_last[t] = weigh(last, t)
     from_below(3, 1)
     from_above(3, 2)
-
-    last = (y + 4) % SLICES
     arrived(chunk(last, 3, first), pair_recv.at[4])
     arrived(chunk(last, 3, second), pair_recv.at[8])
     for t in range(NTAU):
-        gram_occ, gram_vir = grams(last, t)
+        gram_occ, gram_vir = grams(last, t, weighted_last[t])
         out_ref[t] = -((total_occ[t] + gram_occ) * (total_vir[t] + gram_vir))
 
     for build, args in sent:
@@ -462,6 +466,7 @@
             dma,
             pltpu.SemaphoreType.REGULAR,
             dma((SLICES, RUN)),
+            pltpu.VMEM((NTAU, ROWS, WIDTH), bf16),
         ],
         compiler_params=pltpu.CompilerParams(
             collective_id=0, has_side_effects=True, vmem_limit_bytes=40 * 2**20

time: 53.8 us -> 53.7 us (level)
  no operation moved by 1% of the time
where the time goes in v7:
time: 53.7 us; the launch traced here: 53.6 us
  Pallas kernels  52.6 us (98%)
  local copies, waits for them, and re-layouts  0.97 us (2%)
    pallas_call x1, Pallas kernels, local(): pl.pallas_call(gather_and_multiply, out_shape=jax.ShapeDtypeStruct((NTAU,...  52.6 us

profile of v7, /device:TPU:1, one launch (start us, length us, event | category | flops | bytes accessed | tf_op | source)
XLA Modules:
  0.0 53.6 jit_solution(2825465380424360603)
XLA Ops:
  0.0 52.6 %shard_map.55 = f32[2,256,512]{2,1,0:T(8,128)S(1)} custom-call(bf16[16,2048]{1,0:T(8,128)(2,1)} %occ_hbm.1, bf16[16,1024]{1,0:T(8,128)(2,1)} %vir_hbm.1, f32[1,2048]{1,0:T(1,128)} %bitcast.3, f32[1,1024]{1,0:T(1,128)} %bitcast.4, f32[1,2]{1,0:T(1,128)} %bitcast.5), custom_call_target="tpu_custom_call" | custom-call | flops 1610612736 | bytes 2097152 | tf_op jit(solution)/shard_map/pallas_call | solution.py:438
  52.6 1.0 %copy.7 = f32[2,256,512]{2,1,0:T(8,128)} copy(f32[2,256,512]{2,1,0:T(8,128)S(1)} %shard_map.55) | data formatting | bytes 2097152
